TPU v7x, 32 devices: a whole 2x2x4 slice. The times are simulated.
32 devices in a mesh: build: 8 (over z, y), prop: 4 (over x, core).
Axes of the slice: x: 2, y: 2, z: 4, core: 2. Of those that a mesh axis runs over, the one named last changes fastest.
Arguments:
- cholesky: bfloat16 [48, 2048, 2048], P(None, 'build'), may hold values from -0.09375 to 0.09375
- half_vectors: bfloat16 [48, 2048, 128], P(None, 'build'), may hold values from -0.00390625 to 0.00390625
- walkers: bfloat16 [32, 2048, 128], P(('build', 'prop')), may hold values from -6 to 6
- inverse_intersection: bfloat16 [32, 128, 128], P(('build', 'prop')), may hold values from -1.5 to 2.5
- fields: float32 [32, 48], replicated, may hold values from -6 to 6
- weights: float32 [32], replicated, may hold values from 0.5 to 2
- sources: int32 [32], replicated, may hold values from 0 to 31, as said below
Outputs:
- new_walkers: bfloat16 [32, 2048, 128], P(('build', 'prop'))
- new_weights: float32 [32], P(('build', 'prop'))
Inputs may be any that keep to these rules, and one draw needn't show every extreme that they name: sources[w] has the same remainder modulo 4 as w; walkers 0 and 31 continue their own states.
All inputs are finite; a program needn't handle non-finite values.
Results may differ from a plain program's by a relative error of at most 0.014.
Values may be sent and summed in bfloat16 or wider, within the bound.
A program may use at most 192 MiB of HBM per device.

v0:
```python
import jax
import jax.numpy as jnp
from jax import lax
from jax.sharding import PartitionSpec as P

ORDER = 6


def series(potential, begin_state):
    summed = begin_state.astype(jnp.float32)
    current = begin_state
    for degree in range(1, ORDER + 1):
        product = jnp.dot(potential, current, preferred_element_type=jnp.float32) / degree
        summed = summed + product
        current = product.astype(jnp.bfloat16)
    return summed.astype(jnp.bfloat16)


def factors(force_bias, chosen_fields, chosen_weights):
    exponent = jnp.sum(force_bias * (chosen_fields - 0.5 * force_bias), axis=-1)
    return chosen_weights * jnp.exp(exponent)


def shards(cholesky, half_vectors, walkers, inverse_intersection, fields, weights, sources):
    build_count = lax.axis_size("build")
    prop_count = lax.axis_size("prop")
    builder = lax.axis_index("build")
    member = lax.axis_index("prop")
    orbitals = walkers.shape[1]
    electrons = walkers.shape[2]
    vectors = cholesky.shape[0]
    block_rows = orbitals // build_count
    own_state = walkers[0]
    theta_full = jnp.dot(
        own_state, inverse_intersection[0], preferred_element_type=jnp.float32
    ).astype(jnp.bfloat16)
    outgoing = (
        theta_full.reshape(1, build_count, block_rows, electrons),
        own_state.reshape(1, build_count, block_rows, electrons),
    )
    got_theta, got_state = (
        lax.all_to_all(outgoing[0], "build", split_axis=1, concat_axis=0, tiled=True),
        lax.all_to_all(outgoing[1], "build", split_axis=1, concat_axis=0, tiled=True),
    )
    partial_value = jnp.einsum(
        "wri,gri->wg", got_theta[:, 0], half_vectors, preferred_element_type=jnp.float32
    )
    force_bias = lax.psum(partial_value, "build")
    group_fields = lax.dynamic_index_in_dim(
        fields.reshape(build_count, prop_count, vectors), member, 1, False
    )
    group_weights = lax.dynamic_index_in_dim(
        weights.reshape(build_count, prop_count), member, 1, False
    )
    group_sources = (
        lax.dynamic_index_in_dim(sources.reshape(build_count, prop_count), member, 1, False)
        // prop_count
    )
    grown_weights = factors(force_bias, group_fields, group_weights)
    overall = lax.psum(jnp.sum(grown_weights), "prop")
    coeffs = (group_fields - force_bias).astype(jnp.bfloat16)
    picked = jnp.take(coeffs, group_sources, axis=0)
    pot_tiles = jnp.dot(
        picked, cholesky.reshape(vectors, block_rows * orbitals), preferred_element_type=jnp.float32
    )
    pot_tiles = pot_tiles.astype(jnp.bfloat16).reshape(build_count, 1, block_rows, orbitals)
    starts = jnp.take(got_state, group_sources, axis=0)
    potential, begin_state = (
        lax.all_to_all(pot_tiles, "build", split_axis=0, concat_axis=1, tiled=True),
        lax.all_to_all(starts, "build", split_axis=0, concat_axis=1, tiled=True),
    )
    own_source = lax.dynamic_index_in_dim(group_sources, builder, 0, False)
    kept_weight = lax.dynamic_index_in_dim(grown_weights, own_source, 0, False)
    stepped = series(
        potential.reshape(orbitals, orbitals), begin_state.reshape(orbitals, electrons)
    )
    new_weight = kept_weight * (build_count * prop_count) / overall
    return (stepped[None], new_weight.reshape(1))


def solution(mesh):
    placed = (
        P(None, "build", None),
        P(None, "build", None),
        P(("build", "prop"), None, None),
        P(("build", "prop"), None, None),
        P(),
        P(),
        P(),
    )
    return jax.shard_map(
        shards,
        mesh=mesh,
        in_specs=placed,
        out_specs=(P(("build", "prop"), None, None), P(("build", "prop"))),
        check_vma=False,
    )
```

profile of v0, /device:TPU:0, one launch (start us, length us, event | category | flops | bytes accessed | tf_op | source)
XLA Modules:
  0.0 362.1 jit_solution(8123244251063778505)
XLA Ops:
  0.6 0.7 copy-done
  1.4 1.3 convolution_convert_fusion.1
  2.7 0.2 copy.18
  2.9 21.7 %all_to_all.19 = bf16[1,8,256,128]{2,3,0,1:T(8,128)(2,1)} all-to-all(bf16[1,8,256,128]{2,3,0,1:T(8,128)(2,1)S(1)} %copy.18), channel_id=1, replica_groups=mesh['build'=8,'prop'=4] {'build'}, dimensions={1} | all-to-all | bytes 1048576 | tf_op jit(solution)/shard_map/all_to_all | solution.py:42
  24.6 4.1 %all-to-all-start = ((bf16[1,8,256,128]{3,2,0,1:T(8,128)(2,1)}), bf16[1,8,256,128]{3,2,0,1:T(8,128)(2,1)}, u32[]{:S(2)}, u32[]{:S(2)}) async-start(bf16[1,8,256,128]{3,2,0,1:T(8,128)(2,1)} %bitcast.48), calls=%async_computation | async-start | bytes 1048576 | tf_op jit(solution)/shard_map/all_to_all | solution.py:43
  28.8 0.7 reshape.60
  29.5 0.2 and_reduce_fusion
  29.9 3.9 %copy.20 = bf16[48,256,128]{1,0,2:T(8,128)(2,1)S(1)} copy(bf16[48,256,128]{2,1,0:T(8,128)(2,1)} %param.8) | data formatting | bytes 6291456 | tf_op args[1]
  33.7 43.8 %copy.23 = bf16[6,8,256,2048]{3,1,2,0:T(8,128)(2,1)} copy(bf16[6,8,256,2048]{3,2,1,0:T(8,128)(2,1)} %bitcast.44) | data formatting | bytes 100663296
  77.5 0.7 constant_dynamic-slice_fusion
  78.3 1.9 convolution_bitcast_fusion
  80.2 21.7 %psum.14 = f32[8,48]{1,0:T(8,128)S(1)} all-reduce(f32[8,48]{1,0:T(8,128)S(1)} %convolution_bitcast_fusion), channel_id=1, replica_groups=mesh['build'=8,'prop'=4] {'build'}, use_global_device_ids=true, to_apply=%region_0.0 | all-reduce | flops 384 | bytes 3072 | tf_op jit(solution)/shard_map/psum | solution.py:48
  102.1 0.6 gather_fusion.1
  102.6 1.7 gather_fusion
  104.3 0.9 fusion.5
  105.2 3.5 all-to-all-start.1
  108.7 21.5 %convolution_convert_fusion = bf16[8,524288]{1,0:T(8,128)(2,1)} fusion(bf16[48,524288]{1,0:T(8,128)(2,1)} %bitcast.43, bf16[8,48]{1,0:T(8,128)(2,1)S(1)} %gather_fusion.1, pred[8]{0:T(512)(128)(4,1)S(1)} %get-tuple-element.4), kind=kOutput, calls=%fused_computation.2 | convolution fusion | flops 406847872 | bytes 58721032 | tf_op jit(solution)/shard_map/dot_general | solution.py:63
  130.2 11.2 %copy.21 = bf16[8,1,256,2048]{3,2,1,0:T(8,128)(2,1)} copy(bf16[8,1,256,2048]{3,0,2,1:T(8,128)(2,1)} %bitcast.45) | data formatting | bytes 16777216 | tf_op jit(solution)/shard_map/reshape | solution.py:66
  141.4 6.1 %all-to-all-start.3 = ((bf16[8,1,256,2048]{3,2,1,0:T(8,128)(2,1)}), bf16[8,1,256,2048]{3,2,1,0:T(8,128)(2,1)}, u32[]{:S(2)}, u32[]{:S(2)}) async-start(bf16[8,1,256,2048]{3,2,1,0:T(8,128)(2,1)} %copy.21), calls=%async_computation.3 | async-start | bytes 16777216 | tf_op jit(solution)/shard_map/all_to_all | solution.py:69
  147.5 0.2 dynamic-slice_reduce_fusion.1
  147.7 0.6 dynamic_slice.23
  149.7 0.2 dynamic-slice_reduce_fusion
  150.5 0.6 fusion.19
  151.1 6.7 %psum.15 = f32[]{:T(128)} all-reduce(f32[]{:T(128)} %get-tuple-element.2), channel_id=1, replica_groups=mesh['build'=8,'prop'=4] {'prop'}, use_global_device_ids=true, to_apply=%region_3.4 | all-reduce | flops 1 | bytes 8 | tf_op jit(solution)/shard_map/psum | solution.py:60
  157.8 0.6 dynamic_slice.24
  159.7 165.5 %all-to-all-done.3 = bf16[8,1,256,2048]{3,2,1,0:T(8,128)(2,1)} async-done(((bf16[8,1,256,2048]{3,2,1,0:T(8,128)(2,1)}), bf16[8,1,256,2048]{3,2,1,0:T(8,128)(2,1)}, u32[]{:S(2)}, u32[]{:S(2)}) %all-to-all-start.3) | async-done | bytes 8388640 | tf_op jit(solution)/shard_map/all_to_all | solution.py:69
  325.3 5.8 %fusion.20 = f32[2048,128]{1,0:T(8,128)S(1)} fusion(bf16[2048,2048]{1,0:T(8,128)(2,1)} %bitcast.13, bf16[2048,128]{1,0:T(8,128)(2,1)S(1)} %bitcast.46), kind=kOutput, calls=%fused_computation.49 | convolution fusion | flops 1073741824 | bytes 9961472 | tf_op jit(solution)/shard_map/dot_general | solution.py:13
  331.0 5.8 %convolution_multiply_fusion.4 = f32[2048,128]{1,0:T(8,128)S(1)} fusion(bf16[2048,2048]{1,0:T(8,128)(2,1)} %bitcast.13, f32[2048,128]{1,0:T(8,128)S(1)} %fusion.20), kind=kOutput, calls=%fused_computation.7 | convolution fusion | flops 1074266112 | bytes 10485760 | tf_op jit(solution)/shard_map/dot_general | solution.py:13
  336.8 5.8 %convolution_multiply_fusion.3 = f32[2048,128]{1,0:T(8,128)S(1)} fusion(bf16[2048,2048]{1,0:T(8,128)(2,1)} %bitcast.13, f32[2048,128]{1,0:T(8,128)S(1)} %convolution_multiply_fusion.4), kind=kOutput, calls=%fused_computation.6 | convolution fusion | flops 1074266112 | bytes 10485760 | tf_op jit(solution)/shard_map/dot_general | solution.py:13
  342.6 5.8 %convolution_multiply_fusion.2 = f32[2048,128]{1,0:T(8,128)S(1)} fusion(bf16[2048,2048]{1,0:T(8,128)(2,1)} %bitcast.13, f32[2048,128]{1,0:T(8,128)S(1)} %convolution_multiply_fusion.3), kind=kOutput, calls=%fused_computation.5 | convolution fusion | flops 1074266112 | bytes 10485760 | tf_op jit(solution)/shard_map/dot_general | solution.py:13
  348.4 5.8 %convolution_multiply_fusion.1 = f32[2048,128]{1,0:T(8,128)S(1)} fusion(bf16[2048,2048]{1,0:T(8,128)(2,1)} %bitcast.13, f32[2048,128]{1,0:T(8,128)S(1)} %convolution_multiply_fusion.2), kind=kOutput, calls=%fused_computation.4 | convolution fusion | flops 1074266112 | bytes 10485760 | tf_op jit(solution)/shard_map/dot_general | solution.py:13
  354.2 6.8 %fusion.2 = bf16[1,2048,128]{2,1,0:T(8,128)(2,1)} fusion(bf16[2048,2048]{1,0:T(8,128)(2,1)} %bitcast.13, f32[2048,128]{1,0:T(8,128)S(1)} %convolution_multiply_fusion.1, f32[2048,128]{1,0:T(8,128)S(1)} %convolution_multiply_fusion.2, f32[2048,128]{1,0:T(8,128)S(1)} %convolution_multiply_fusion.3, f32[2048,128]{1,0:T(8,128)S(1)} %convolution_multiply_fusion.4, ...), kind=kOutput, calls=%fused_computation.11 | convolution fusion | flops 1076363264 | bytes 14680064 | tf_op jit(solution)/shard_map/dot_general | solution.py:13
  (12 shorter events, 0.4 us)
Async XLA Ops:
  0.6 0.8 copy-start
  24.6 78.0 %all-to-all-start = ((bf16[1,8,256,128]{3,2,0,1:T(8,128)(2,1)}), bf16[1,8,256,128]{3,2,0,1:T(8,128)(2,1)}, u32[]{:S(2)}, u32[]{:S(2)}) async-start(bf16[1,8,256,128]{3,2,0,1:T(8,128)(2,1)} %bitcast.48), calls=%async_computation | async-start | bytes 1048576 | tf_op jit(solution)/shard_map/all_to_all | solution.py:43
  105.2 36.2 %all-to-all-start.1 = ((bf16[8,1,256,128]{3,2,1,0:T(8,128)(2,1)}), bf16[8,1,256,128]{3,2,1,0:T(8,128)(2,1)S(1)}, u32[]{:S(2)}, u32[]{:S(2)}) async-start(bf16[8,1,256,128]{3,2,1,0:T(8,128)(2,1)} %fusion.5), calls=%async_computation.1 | async-start | bytes 1048576 | tf_op jit(solution)/shard_map/all_to_all | solution.py:70
  141.4 8.1 %copy-start.2 = (f32[32]{0:T(128)S(1)}, f32[32]{0:T(128)}, u32[]{:S(2)}) copy-start(f32[32]{0:T(128)} %param.12) | copy-start | bytes 388
  141.4 183.8 %all-to-all-start.3 = ((bf16[8,1,256,2048]{3,2,1,0:T(8,128)(2,1)}), bf16[8,1,256,2048]{3,2,1,0:T(8,128)(2,1)}, u32[]{:S(2)}, u32[]{:S(2)}) async-start(bf16[8,1,256,2048]{3,2,1,0:T(8,128)(2,1)} %copy.21), calls=%async_computation.3 | async-start | bytes 16777216 | tf_op jit(solution)/shard_map/all_to_all | solution.py:69
  348.4 12.6 %copy-start.1 = (bf16[1,128,128]{2,1,0:T(8,128)(2,1)S(1)}, bf16[1,128,128]{2,1,0:T(8,128)(2,1)}, u32[]{:S(2)}) copy-start(bf16[1,128,128]{2,1,0:T(8,128)(2,1)} %param.10) | copy-start | bytes 98308
where the time goes:
time: 363 us; the launch traced here: 362 us
  waiting for transfers between devices  166 us (46%)
  local copies, waits for them, and re-layouts  65.2 us (18%)
  matrix products  60.4 us (17%)
  blocking collectives  50.1 us (14%)
  starting transfers between devices  13.7 us (4%)
  between operations  5.18 us (1%)
    all_to_all x1, waiting for transfers between devices, shards(): lax.all_to_all(pot_tiles, 'build', split_axis=0, concat_axis=1, tiled=True)  166 us
    unnamed x8, local copies, waits for them, and re-layouts  48.4 us
    dot_general x6, matrix products, series(): jnp.dot(potential, current, preferred_element_type=jnp.float32) / degree  35.6 us
    psum x1, blocking collectives, shards(): force_bias = lax.psum(partial_value, 'build')  21.7 us
    all_to_all x1, blocking collectives, shards(): lax.all_to_all(outgoing[0], 'build', split_axis=1, concat_axis=0, tiled=T...  21.7 us
    dot_general x1, matrix products, shards(): jnp.dot(picked, cholesky.reshape(vectors, block_rows * orbitals), preferr...  21.5 us
    reshape x1, local copies, waits for them, and re-layouts, shards(): pot_tiles.astype(jnp.bfloat16).reshape(build_count, 1, block_rows, orbitals)  11.2 us
  transfers between devices with their start and end apart: 3, of which 1 were waited for; matrix products, arithmetic and copies ran while one was open for 24% of the time, Pallas kernels for 0%

commit v1 on v0

--- a/solution.py
+++ b/solution.py
@@ -1,19 +1,293 @@
+import functools
+
 import jax
 import jax.numpy as jnp
 from jax import lax
+from jax.experimental import pallas as pl
+from jax.experimental.pallas import tpu as pltpu
 from jax.sharding import PartitionSpec as P
 
 ORDER = 6
-
-
-def series(potential, begin_state):
-    summed = begin_state.astype(jnp.float32)
-    current = begin_state
-    for degree in range(1, ORDER + 1):
-        product = jnp.dot(potential, current, preferred_element_type=jnp.float32) / degree
-        summed = summed + product
-        current = product.astype(jnp.bfloat16)
-    return summed.astype(jnp.bfloat16)
+TILE = 16
+SLOTS = 4
+MESH = pl.DeviceIdType.MESH
+f32 = jnp.float32
+bf16 = jnp.bfloat16
+
+
+def spread(coeffs, vectors):
+    count = coeffs.shape[0]
+    wide = vectors * TILE
+    lane = lax.broadcasted_iota(jnp.int32, (vectors, wide), 1) // TILE
+    row = lax.broadcasted_iota(jnp.int32, (vectors, wide), 0)
+    repeat_columns = (lane == row).astype(f32).astype(bf16)
+    line = lax.broadcasted_iota(jnp.int32, (count * TILE, count), 0) // TILE
+    walker = lax.broadcasted_iota(jnp.int32, (count * TILE, count), 1)
+    repeat_rows = (line == walker).astype(f32).astype(bf16)
+    along = jnp.dot(coeffs, repeat_columns, preferred_element_type=f32).astype(bf16)
+    both = jnp.dot(repeat_rows, along, preferred_element_type=f32)
+    at_row = lax.broadcasted_iota(jnp.int32, (count * TILE, wide), 0) % TILE
+    at_lane = lax.broadcasted_iota(jnp.int32, (count * TILE, wide), 1) % TILE
+    return jnp.where(at_row == at_lane, both, 0.0).astype(bf16)
+
+
+def step_kernel(
+    nb,
+    picked_ref,
+    starts_ref,
+    chol_ref,
+    out_ref,
+    chunks,
+    mixer,
+    tiles,
+    pot,
+    terms,
+    summed,
+    finals,
+    landed,
+    load_sem,
+    self_sem,
+    pot_send,
+    pot_recv,
+    state_send,
+    state_recv,
+    term_send,
+    term_recv,
+    last_send,
+    last_recv,
+):
+    me = lax.axis_index("build")
+    nh = nb // 2
+    half = me // nh
+    place = lax.rem(me, nh)
+    peer = lax.rem(me + nh, nb)
+    vectors, br, orbitals = chol_ref.shape
+    hr = orbitals // 2
+    row_tiles = br // TILE
+    group = min(nb, 8)
+    cols = min(orbitals, 512)
+    rows = min(hr, 256)
+
+    def load(t):
+        slot = lax.rem(t, SLOTS)
+        return pltpu.make_async_copy(
+            chol_ref.at[:, pl.ds(t * TILE, TILE), :], chunks.at[slot], load_sem.at[slot]
+        )
+
+    for t in range(min(SLOTS - 1, row_tiles)):
+        load(jnp.int32(t)).start()
+
+    barrier = pltpu.get_barrier_semaphore()
+
+    def greet(j, carry):
+        pl.semaphore_signal(
+            barrier, inc=1, device_id={"build": lax.rem(me + j, nb)}, device_id_type=MESH
+        )
+        return carry
+
+    lax.fori_loop(1, nb, greet, 0)
+
+    def fill(v, carry):
+        c = picked_ref[pl.ds(v * group, group), :]
+        mixer[pl.ds(v * group * TILE, group * TILE), :] = spread(c, vectors)
+        return carry
+
+    lax.fori_loop(0, nb // group, fill, 0)
+    own_rows = pl.ds(me * br, br)
+    for s in range(2):
+        terms[0, s, own_rows, :] = starts_ref[place + s * nh]
+    pl.semaphore_wait(barrier, nb - 1)
+
+    def send_pot(s, j, first, count):
+        to = lax.rem(place + j, nh)
+        return pltpu.make_async_remote_copy(
+            src_ref=tiles.at[to + s * nh, pl.ds(first, count)],
+            dst_ref=pot.at[s, pl.ds(place * br + first, count)],
+            send_sem=pot_send.at[s],
+            recv_sem=pot_recv.at[s],
+            device_id={"build": half * nh + to},
+            device_id_type=MESH,
+        )
+
+    def send_state(s, j):
+        to = lax.rem(me + j, nb)
+        return pltpu.make_async_remote_copy(
+            src_ref=starts_ref.at[lax.rem(to, nh) + s * nh],
+            dst_ref=terms.at[0, s, own_rows],
+            send_sem=state_send.at[s],
+            recv_sem=state_recv.at[s],
+            device_id={"build": to},
+            device_id_type=MESH,
+        )
+
+    def block(t, carry):
+        slot = lax.rem(t, SLOTS)
+
+        @pl.when(t + SLOTS - 1 < row_tiles)
+        def _():
+            load(t + SLOTS - 1).start()
+
+        load(t).wait()
+
+        def part(i, inner):
+            v = i // (orbitals // cols)
+            c = lax.rem(i, orbitals // cols) * cols
+            c = pl.multiple_of(c, cols)
+            right = chunks[slot, :, :, pl.ds(c, cols)].reshape(vectors * TILE, cols)
+            left = mixer[pl.ds(v * group * TILE, group * TILE), :]
+            made = jnp.dot(left, right, preferred_element_type=f32).astype(bf16)
+            tiles[pl.ds(v * group, group), pl.ds(t * TILE, TILE), pl.ds(c, cols)] = (
+                made.reshape(group, TILE, cols)
+            )
+            return inner
+
+        lax.fori_loop(0, (nb // group) * (orbitals // cols), part, 0)
+
+        def push(j, inner):
+            send_pot(0, j, t * TILE, TILE).start()
+            return inner
+
+        lax.fori_loop(1, nh, push, 0)
+        return carry
+
+    lax.fori_loop(0, row_tiles, block, 0)
+
+    for s in range(2):
+
+        def push_state(j, carry):
+            send_state(s, j).start()
+            return carry
+
+        lax.fori_loop(1, nb, push_state, 0)
+
+    def keep(s):
+        return pltpu.make_async_copy(
+            tiles.at[place + s * nh], pot.at[s, pl.ds(place * br, br)], self_sem.at[s]
+        )
+
+    for s in range(2):
+        keep(s).start()
+
+    def others(ref, sem, count):
+        return pltpu.make_async_copy(ref.at[pl.ds(0, count)], ref.at[pl.ds(0, count)], sem)
+
+    far = (nh - 1) * br
+    others(pot.at[0], pot_send.at[0], far).wait()
+
+    def push_rest(j, carry):
+        send_pot(1, j, 0, br).start()
+        return carry
+
+    lax.fori_loop(1, nh, push_rest, 0)
+
+    def send_term(k, s, first):
+        at = pl.ds(half * hr + first, rows)
+        return pltpu.make_async_remote_copy(
+            src_ref=terms.at[k, s, at],
+            dst_ref=terms.at[k, s, at],
+            send_sem=term_send.at[k, s],
+            recv_sem=term_recv.at[k, s],
+            device_id={"build": peer},
+            device_id_type=MESH,
+        )
+
+    def send_last(s, first):
+        return pltpu.make_async_remote_copy(
+            src_ref=finals.at[s, pl.ds(first, rows)],
+            dst_ref=landed.at[pl.ds(first, rows)],
+            send_sem=last_send,
+            recv_sem=last_recv,
+            device_id={"build": peer},
+            device_id_type=MESH,
+        )
+
+    def advance(k, s):
+        if k == 1:
+            others(terms.at[0, s], state_recv.at[s], (nb - 1) * br).wait()
+            keep(s).wait()
+            others(pot.at[s], pot_recv.at[s], far).wait()
+        else:
+            others(terms.at[k - 1, s], term_recv.at[k - 1, s], hr).wait()
+
+        def piece(i, carry):
+            first = pl.multiple_of(i * rows, rows)
+            at = pl.ds(first, rows)
+            here = pl.ds(pl.multiple_of(half * hr + first, rows), rows)
+            product = jnp.dot(pot[s, at, :], terms[k - 1, s], preferred_element_type=f32) / k
+            if k == 1:
+                total = terms[0, s, here, :].astype(f32) + product
+            else:
+                total = summed[s, at, :] + product
+            if k < ORDER:
+                summed[s, at, :] = total
+                terms[k, s, here, :] = product.astype(bf16)
+                send_term(k, s, first).start()
+            else:
+                finals[s, at, :] = total.astype(bf16)
+
+                @pl.when(half != s)
+                def _():
+                    send_last(s, first).start()
+
+            return carry
+
+        lax.fori_loop(0, hr // rows, piece, 0)
+
+    lead = 3
+    for k in range(1, lead + 1):
+        advance(k, 0)
+    for k in range(1, ORDER + 1):
+        advance(k, 1)
+        if k + lead <= ORDER:
+            advance(k + lead, 0)
+
+    own_half = pl.ds(pl.multiple_of(half * hr, hr), hr)
+    out_ref[own_half, :] = finals[half]
+    others(landed, last_recv, hr).wait()
+    other_half = pl.ds(pl.multiple_of((1 - half) * hr, hr), hr)
+    out_ref[other_half, :] = landed[...]
+    others(landed, last_send, hr).wait()
+    others(pot.at[1], pot_send.at[1], far).wait()
+    for s in range(2):
+        others(terms.at[0, s], state_send.at[s], (nb - 1) * br).wait()
+        for k in range(1, ORDER):
+            others(terms.at[k, s], term_send.at[k, s], hr).wait()
+
+
+def propagate(nb, picked, starts, cholesky):
+    vectors, br, orbitals = cholesky.shape
+    electrons = starts.shape[2]
+    hr = orbitals // 2
+    vmem = pl.BlockSpec(memory_space=pltpu.VMEM)
+    return pl.pallas_call(
+        functools.partial(step_kernel, nb),
+        out_shape=jax.ShapeDtypeStruct((orbitals, electrons), bf16),
+        in_specs=[vmem, vmem, pl.BlockSpec(memory_space=pl.ANY)],
+        out_specs=vmem,
+        scratch_shapes=[
+            pltpu.VMEM((SLOTS, vectors, TILE, orbitals), bf16),
+            pltpu.VMEM((nb * TILE, vectors * TILE), bf16),
+            pltpu.VMEM((nb, br, orbitals), bf16),
+            pltpu.VMEM((2, hr, orbitals), bf16),
+            pltpu.VMEM((ORDER, 2, orbitals, electrons), bf16),
+            pltpu.VMEM((2, hr, electrons), f32),
+            pltpu.VMEM((2, hr, electrons), bf16),
+            pltpu.VMEM((hr, electrons), bf16),
+            pltpu.SemaphoreType.DMA((SLOTS,)),
+            pltpu.SemaphoreType.DMA((2,)),
+            pltpu.SemaphoreType.DMA((2,)),
+            pltpu.SemaphoreType.DMA((2,)),
+            pltpu.SemaphoreType.DMA((2,)),
+            pltpu.SemaphoreType.DMA((2,)),
+            pltpu.SemaphoreType.DMA((ORDER, 2)),
+            pltpu.SemaphoreType.DMA((ORDER, 2)),
+            pltpu.SemaphoreType.DMA,
+            pltpu.SemaphoreType.DMA,
+        ],
+        compiler_params=pltpu.CompilerParams(
+            collective_id=0, has_side_effects=True, vmem_limit_bytes=56 * 1024 * 1024
+        ),
+    )(picked, starts, cholesky)
 
 
 def factors(force_bias, chosen_fields, chosen_weights):
@@ -60,20 +334,10 @@
     overall = lax.psum(jnp.sum(grown_weights), "prop")
     coeffs = (group_fields - force_bias).astype(jnp.bfloat16)
     picked = jnp.take(coeffs, group_sources, axis=0)
-    pot_tiles = jnp.dot(
-        picked, cholesky.reshape(vectors, block_rows * orbitals), preferred_element_type=jnp.float32
-    )
-    pot_tiles = pot_tiles.astype(jnp.bfloat16).reshape(build_count, 1, block_rows, orbitals)
-    starts = jnp.take(got_state, group_sources, axis=0)
-    potential, begin_state = (
-        lax.all_to_all(pot_tiles, "build", split_axis=0, concat_axis=1, tiled=True),
-        lax.all_to_all(starts, "build", split_axis=0, concat_axis=1, tiled=True),
-    )
+    starts = jnp.take(got_state[:, 0], group_sources, axis=0)
+    stepped = propagate(build_count, picked, starts, cholesky)
     own_source = lax.dynamic_index_in_dim(group_sources, builder, 0, False)
     kept_weight = lax.dynamic_index_in_dim(grown_weights, own_source, 0, False)
-    stepped = series(
-        potential.reshape(orbitals, orbitals), begin_state.reshape(orbitals, electrons)
-    )
     new_weight = kept_weight * (build_count * prop_count) / overall
     return (stepped[None], new_weight.reshape(1))
 

time: 363 us -> 311 us (0.86)
  Pallas kernels: 0 us -> 233 us
  waiting for transfers between devices: 166 us -> 14.2 us
  matrix products: 60.4 us -> 3.27 us
  local copies, waits for them, and re-layouts: 65.2 us -> 12.2 us
  blocking collectives: 50.1 us -> 28 us
    pallas_call x0 -> x1, Pallas kernels: none -> 233 us  [propagate(): pl.pallas_call(functools.partial(step_kernel, nb), out_shape=jax.ShapeDty...]
    all_to_all x2 -> x1, waiting for transfers between devices: 166 us -> 14.2 us  [shards(): lax.all_to_all(outgoing[0], 'build', split_axis=1, concat_axis=0, tiled=T...]
    dot_general x7 -> x0, matrix products: 57.1 us -> none  [the longest x6 35.6 us: series(): jnp.dot(potential, current, preferred_element_type=jnp.float32) / degree]
    unnamed x8 -> x10, local copies, waits for them, and re-layouts: 48.4 us -> 6.49 us
    all_to_all x1 -> x0, blocking collectives: 21.7 us -> none  [shards(): lax.all_to_all(outgoing[0], 'build', split_axis=1, concat_axis=0, tiled=T...]
    reshape x1 -> x0, local copies, waits for them, and re-layouts: 11.2 us -> none  [shards(): pot_tiles.astype(jnp.bfloat16).reshape(build_count, 1, block_rows, orbitals)]
    all_to_all x2 -> x1, starting transfers between devices: 9.55 us -> 7.28 us  [shards(): lax.all_to_all(outgoing[0], 'build', split_axis=1, concat_axis=0, tiled=T...]
  transfers between devices with their start and end apart: 3 -> 2, of which waited for: 1 -> 1; matrix products, arithmetic and copies ran while one was open for 24% -> 3% of each run, Pallas kernels for 0% -> 0%
where the time goes in v1:
time: 311 us; the launch traced here: 310 us
  Pallas kernels  233 us (75%)
  blocking collectives  28 us (9%)
  waiting for transfers between devices  14.2 us (5%)
  local copies, waits for them, and re-layouts  12.2 us (4%)
  starting transfers between devices  11.4 us (4%)
  between operations  5.16 us (2%)
  matrix products  3.27 us (1%)
    pallas_call x1, Pallas kernels, propagate(): pl.pallas_call(functools.partial(step_kernel, nb), out_shape=jax.ShapeDty...  233 us
    psum x1, blocking collectives, shards(): force_bias = lax.psum(partial_value, 'build')  21.7 us
    all_to_all x1, waiting for transfers between devices, shards(): lax.all_to_all(outgoing[0], 'build', split_axis=1, concat_axis=0, tiled=T...  14.2 us
    all_to_all x1, starting transfers between devices, shards(): lax.all_to_all(outgoing[0], 'build', split_axis=1, concat_axis=0, tiled=T...  7.28 us
    unnamed x10, local copies, waits for them, and re-layouts  6.49 us
    psum x1, blocking collectives, shards(): overall = lax.psum(jnp.sum(grown_weights), 'prop')  6.27 us
  transfers between devices with their start and end apart: 2, of which 1 were waited for; matrix products, arithmetic and copies ran while one was open for 3% of the time, Pallas kernels for 0%

profile of v1, /device:TPU:0, one launch (start us, length us, event | category | flops | bytes accessed | tf_op | source)
XLA Modules:
  0.0 310.1 jit_solution(8829033168808646124)
XLA Ops:
  0.6 0.0 copy-start
  0.6 0.0 copy-start.2
  0.7 0.7 copy-done
  1.4 1.3 convolution_convert_fusion
  2.7 1.0 copy.16
  3.7 7.3 %all-to-all-start = ((bf16[1,8,256,128]{2,3,0,1:T(8,128)(2,1)}), bf16[1,8,256,128]{2,3,0,1:T(8,128)(2,1)S(1)}, u32[]{:S(2)}, u32[]{:S(2)}) async-start(bf16[1,8,256,128]{2,3,0,1:T(8,128)(2,1)} %copy.16), calls=%async_computation | async-start | bytes 1048576 | tf_op jit(solution)/shard_map/all_to_all | solution.py:316
  11.0 0.1 reshape.33
  11.1 0.2 dynamic-slice_reduce_fusion.1
  11.3 14.2 %all-to-all-done = bf16[1,8,256,128]{2,3,0,1:T(8,128)(2,1)S(1)} async-done(((bf16[1,8,256,128]{2,3,0,1:T(8,128)(2,1)}), bf16[1,8,256,128]{2,3,0,1:T(8,128)(2,1)S(1)}, u32[]{:S(2)}, u32[]{:S(2)}) %all-to-all-start) | async-done | bytes 524320 | tf_op jit(solution)/shard_map/all_to_all | solution.py:316
  25.5 4.1 %all-to-all-start.1 = ((bf16[1,8,256,128]{3,2,0,1:T(8,128)(2,1)}), bf16[1,8,256,128]{3,2,0,1:T(8,128)(2,1)}, u32[]{:S(2)}, u32[]{:S(2)}) async-start(bf16[1,8,256,128]{3,2,0,1:T(8,128)(2,1)} %bitcast.7), calls=%async_computation.1 | async-start | bytes 1048576 | tf_op jit(solution)/shard_map/all_to_all | solution.py:317
  29.7 0.6 dynamic_slice.23
  31.6 0.0 copy-start.3
  31.6 3.9 %copy.18 = bf16[48,256,128]{1,0,2:T(8,128)(2,1)S(1)} copy(bf16[48,256,128]{2,1,0:T(8,128)(2,1)} %param.8) | data formatting | bytes 6291456 | tf_op args[1]
  35.5 0.2 and_reduce_fusion
  35.7 0.1 reduce.1
  35.8 0.0 copy-done.3
  35.8 0.1 reshape.36
  35.9 0.2 dynamic-slice_reduce_fusion
  36.7 0.7 constant_dynamic-slice_fusion
  37.4 2.0 convolution_bitcast_fusion
  39.4 21.7 %psum.14 = f32[8,48]{1,0:T(8,128)S(1)} all-reduce(f32[8,48]{1,0:T(8,128)S(1)} %convolution_bitcast_fusion), channel_id=1, replica_groups=mesh['build'=8,'prop'=4] {'build'}, use_global_device_ids=true, to_apply=%region_0.0 | all-reduce | flops 384 | bytes 3072 | tf_op jit(solution)/shard_map/psum | solution.py:322
  61.1 0.1 multiply_reduce_fusion
  61.3 0.6 gather_fusion
  61.8 0.0 all-to-all-done.1
  61.8 1.7 gather_fusion.1
  63.5 0.7 broadcast_select_fusion.1.picked_ref
  64.2 0.9 broadcast_select_fusion.starts_ref
  65.1 233.2 %shard_map.86 = bf16[2048,128]{1,0:T(8,128)(2,1)} custom-call(bf16[8,48]{1,0:T(8,128)(2,1)} %broadcast_select_fusion.1.picked_ref, bf16[8,256,128]{2,1,0:T(8,128)(2,1)} %broadcast_select_fusion.starts_ref, bf16[48,256,2048]{2,1,0:T(8,128)(2,1)} %chol_ref.1), custom_call_target="tpu_custom_call" | custom-call | tf_op jit(solution)/shard_map/pallas_call | solution.py:262
  298.3 0.6 fusion.6
  299.0 6.3 %psum.15 = f32[]{:T(128)} all-reduce(f32[]{:T(128)} %get-tuple-element.2), channel_id=1, replica_groups=mesh['build'=8,'prop'=4] {'prop'}, use_global_device_ids=true, to_apply=%region_3.4 | all-reduce | flops 1 | bytes 8 | tf_op jit(solution)/shard_map/psum | solution.py:334
  305.2 0.6 dynamic_slice.24
  307.1 1.9 copy.25
  (5 shorter events, 0.0 us)
Async XLA Ops:
  0.6 0.8 copy-start
  0.6 10.4 %copy-start.2 = (s32[32]{0:T(128)S(1)}, s32[32]{0:T(128)}, u32[]{:S(2)}) copy-start(s32[32]{0:T(128)} %param.13) | copy-start | bytes 388
  3.7 21.8 %all-to-all-start = ((bf16[1,8,256,128]{2,3,0,1:T(8,128)(2,1)}), bf16[1,8,256,128]{2,3,0,1:T(8,128)(2,1)S(1)}, u32[]{:S(2)}, u32[]{:S(2)}) async-start(bf16[1,8,256,128]{2,3,0,1:T(8,128)(2,1)} %copy.16), calls=%async_computation | async-start | bytes 1048576 | tf_op jit(solution)/shard_map/all_to_all | solution.py:316
  25.5 5.4 %copy-start.1 = (bf16[1,8,256,128]{2,3,0,1:T(8,128)(2,1)}, bf16[1,8,256,128]{2,3,0,1:T(8,128)(2,1)S(1)}, u32[]{:S(2)}) copy-start(bf16[1,8,256,128]{2,3,0,1:T(8,128)(2,1)S(1)} %all-to-all-done) | copy-start | bytes 1572868
  25.5 36.3 %all-to-all-start.1 = ((bf16[1,8,256,128]{3,2,0,1:T(8,128)(2,1)}), bf16[1,8,256,128]{3,2,0,1:T(8,128)(2,1)}, u32[]{:S(2)}, u32[]{:S(2)}) async-start(bf16[1,8,256,128]{3,2,0,1:T(8,128)(2,1)} %bitcast.7), calls=%async_computation.1 | async-start | bytes 1048576 | tf_op jit(solution)/shard_map/all_to_all | solution.py:317
  31.6 4.2 %copy-start.3 = (f32[32]{0:T(128)S(1)}, f32[32]{0:T(128)}, u32[]{:S(2)}) copy-start(f32[32]{0:T(128)} %param.12) | copy-start | bytes 388

commit v2 on v1

v2 whole, which is shorter than its diff:
```python
import functools

import jax
import jax.numpy as jnp
from jax import lax
from jax.experimental import pallas as pl
from jax.experimental.pallas import tpu as pltpu
from jax.sharding import PartitionSpec as P

ORDER = 6
TILE = 16
SLOTS = 4
MESH = pl.DeviceIdType.MESH
f32 = jnp.float32
bf16 = jnp.bfloat16


def spread(coeffs, wide):
    count, vectors = coeffs.shape
    lane = lax.broadcasted_iota(jnp.int32, (vectors, wide), 1) // TILE
    row = lax.broadcasted_iota(jnp.int32, (vectors, wide), 0)
    repeat_columns = (lane == row).astype(f32).astype(bf16)
    line = lax.broadcasted_iota(jnp.int32, (count * TILE, count), 0) // TILE
    walker = lax.broadcasted_iota(jnp.int32, (count * TILE, count), 1)
    repeat_rows = (line == walker).astype(f32).astype(bf16)
    along = jnp.dot(coeffs, repeat_columns, preferred_element_type=f32).astype(bf16)
    both = jnp.dot(repeat_rows, along, preferred_element_type=f32)
    at_row = lax.broadcasted_iota(jnp.int32, (count * TILE, wide), 0) % TILE
    at_lane = lax.broadcasted_iota(jnp.int32, (count * TILE, wide), 1) % TILE
    return jnp.where(at_row == at_lane, both, 0.0).astype(bf16)


def step_kernel(
    nb,
    npr,
    walker_ref,
    inverse_ref,
    half_ref,
    fields_ref,
    weights_ref,
    choice_ref,
    origin_ref,
    chol_ref,
    out_ref,
    grown_ref,
    overall_ref,
    got,
    inverses,
    theta,
    mixed,
    parts,
    sums,
    picked_ref,
    starts_ref,
    chunks,
    mixer,
    tiles,
    pot,
    terms,
    summed,
    finals,
    landed,
    load_sem,
    self_sem,
    got_send,
    got_recv,
    inverse_send,
    inverse_recv,
    part_send,
    part_recv,
    sum_send,
    sum_recv,
    pot_send,
    pot_recv,
    state_send,
    state_recv,
    term_send,
    term_recv,
    last_send,
    last_recv,
):
    me = lax.axis_index("build")
    mine = lax.axis_index("prop")
    nh = nb // 2
    half = me // nh
    place = lax.rem(me, nh)
    peer = lax.rem(me + nh, nb)
    vectors, br, orbitals = chol_ref.shape
    electrons = walker_ref.shape[1]
    wide = vectors * TILE
    lanes = fields_ref.shape[1]
    hr = orbitals // 2
    row_tiles = br // TILE
    slots = chunks.shape[0]
    group = min(nb, 8)
    cols = min(orbitals, 512)
    rows = min(hr, 512)
    pieces = min(4, row_tiles)

    def load(t):
        slot = lax.rem(t, slots)
        return pltpu.make_async_copy(
            chol_ref.at[:, pl.ds(t * TILE, TILE), :], chunks.at[slot], load_sem.at[slot]
        )

    def others(ref, sem, count):
        return pltpu.make_async_copy(ref.at[pl.ds(0, count)], ref.at[pl.ds(0, count)], sem)

    barrier = pltpu.get_barrier_semaphore()

    def greet(j, carry):
        pl.semaphore_signal(
            barrier, inc=1, device_id={"build": lax.rem(me + j, nb)}, device_id_type=MESH
        )
        return carry

    lax.fori_loop(1, nb, greet, 0)
    for j in range(1, npr):
        pl.semaphore_signal(
            barrier, inc=1, device_id={"prop": lax.rem(mine + j, npr)}, device_id_type=MESH
        )
    for t in range(min(slots, row_tiles)):
        load(jnp.int32(t)).start()
    own_rows = pl.ds(pl.multiple_of(me * br, br), br)
    got[me] = walker_ref[own_rows, :]
    inverses[me] = inverse_ref[...]
    pl.semaphore_wait(barrier, nb - 1 + npr - 1)

    def share(j, carry):
        to = lax.rem(me + j, nb)
        pltpu.make_async_remote_copy(
            src_ref=inverse_ref,
            dst_ref=inverses.at[me],
            send_sem=inverse_send,
            recv_sem=inverse_recv,
            device_id={"build": to},
            device_id_type=MESH,
        ).start()
        pltpu.make_async_remote_copy(
            src_ref=walker_ref.at[pl.ds(to * br, br)],
            dst_ref=got.at[me],
            send_sem=got_send,
            recv_sem=got_recv,
            device_id={"build": to},
            device_id_type=MESH,
        ).start()
        return carry

    lax.fori_loop(1, nb, share, 0)
    others(inverses, inverse_recv, nb - 1).wait()
    others(got, got_recv, nb - 1).wait()

    def rotate(v, carry):
        theta[v] = jnp.dot(got[v], inverses[v], preferred_element_type=f32).astype(bf16)
        starts_ref[v] = got[origin_ref[v]]
        return carry

    lax.fori_loop(0, nb, rotate, 0)

    def bias(u, carry):
        first = pl.multiple_of(u * group, group)
        mixed[...] = jnp.zeros_like(mixed)

        def add(t, inner):
            at = pl.ds(pl.multiple_of(t * TILE, TILE), TILE)
            left = theta[pl.ds(first, group), at, :].reshape(group * TILE, electrons)
            right = half_ref[:, at, :].reshape(wide, electrons)
            mixed[...] += lax.dot_general(
                left, right, (((1,), (1,)), ((), ())), preferred_element_type=f32
            )
            return inner

        lax.fori_loop(0, row_tiles, add, 0)
        at_row = lax.broadcasted_iota(jnp.int32, (group * TILE, wide), 0) % TILE
        at_lane = lax.broadcasted_iota(jnp.int32, (group * TILE, wide), 1) % TILE
        kept = jnp.where(at_row == at_lane, mixed[...], 0.0)
        short = jnp.sum(kept.reshape(group, TILE, wide), axis=1)
        source = lax.broadcasted_iota(jnp.int32, (wide, lanes), 0) // TILE
        target = lax.broadcasted_iota(jnp.int32, (wide, lanes), 1)
        gather = (source == target).astype(f32)
        parts[me, pl.ds(first, group), :] = jnp.dot(
            short, gather, precision=lax.Precision.HIGHEST, preferred_element_type=f32
        )
        return carry

    lax.fori_loop(0, nb // group, bias, 0)

    def tell(j, carry):
        pltpu.make_async_remote_copy(
            src_ref=parts.at[me],
            dst_ref=parts.at[me],
            send_sem=part_send,
            recv_sem=part_recv,
            device_id={"build": lax.rem(me + j, nb)},
            device_id_type=MESH,
        ).start()
        return carry

    lax.fori_loop(1, nb, tell, 0)

    def send_state(s, j):
        to = lax.rem(me + j, nb)
        return pltpu.make_async_remote_copy(
            src_ref=starts_ref.at[lax.rem(to, nh) + s * nh],
            dst_ref=terms.at[0, s, own_rows],
            send_sem=state_send.at[s],
            recv_sem=state_recv.at[s],
            device_id={"build": to},
            device_id_type=MESH,
        )

    def push_states(s):
        def push_state(j, carry):
            send_state(s, j).start()
            return carry

        lax.fori_loop(1, nb, push_state, 0)

    push_states(0)
    for s in range(2):
        terms[0, s, own_rows, :] = starts_ref[place + s * nh]
    others(parts, part_recv, nb - 1).wait()
    force_bias = lax.fori_loop(
        1, nb, lambda j, held: held + parts[j], parts[0]
    )
    drawn = fields_ref[...]
    exponent = jnp.sum(force_bias * (drawn - 0.5 * force_bias), axis=-1, keepdims=True)
    grown = weights_ref[...] * jnp.exp(exponent)
    grown_ref[...] = grown
    sums[mine] = jnp.broadcast_to(jnp.sum(grown, axis=0, keepdims=True), sums.shape[1:])
    for j in range(1, npr):
        pltpu.make_async_remote_copy(
            src_ref=sums.at[mine],
            dst_ref=sums.at[mine],
            send_sem=sum_send,
            recv_sem=sum_recv,
            device_id={"prop": lax.rem(mine + j, npr)},
            device_id_type=MESH,
        ).start()
    coeffs = (drawn - force_bias).astype(bf16)
    picked_ref[...] = jnp.dot(choice_ref[...], coeffs, preferred_element_type=f32)

    def fill(v, carry):
        c = picked_ref[pl.ds(pl.multiple_of(v * group, group), group), :].astype(bf16)
        at = pl.ds(pl.multiple_of(v * group * TILE, group * TILE), group * TILE)
        mixer[at, :] = spread(c, wide)
        return carry

    if nb == group:
        mixer[...] = spread(picked_ref[...].astype(bf16), wide)
    else:
        lax.fori_loop(0, nb // group, fill, 0)

    def send_pot(s, j, first, count):
        to = lax.rem(place + j, nh)
        return pltpu.make_async_remote_copy(
            src_ref=tiles.at[to + s * nh, pl.ds(first, count)],
            dst_ref=pot.at[s, pl.ds(place * br + first, count)],
            send_sem=pot_send.at[s],
            recv_sem=pot_recv.at[s],
            device_id={"build": half * nh + to},
            device_id_type=MESH,
        )

    def block(t, carry):
        slot = lax.rem(t, slots)
        load(t).wait()

        def part(i, inner):
            v = i // (orbitals // cols)
            c = lax.rem(i, orbitals // cols) * cols
            c = pl.multiple_of(c, cols)
            right = chunks[slot, :, :, pl.ds(c, cols)].reshape(vectors * TILE, cols)
            left = mixer[pl.ds(pl.multiple_of(v * group * TILE, group * TILE), group * TILE), :]
            made = jnp.dot(left, right, preferred_element_type=f32).astype(bf16)
            tiles[pl.ds(v * group, group), pl.ds(pl.multiple_of(t * TILE, TILE), TILE), pl.ds(c, cols)] = (
                made.reshape(group, TILE, cols)
            )
            return inner

        lax.fori_loop(0, (nb // group) * (orbitals // cols), part, 0)

        @pl.when(t + slots < row_tiles)
        def _():
            load(t + slots).start()

        def push(j, inner):
            send_pot(0, j, t * TILE, TILE).start()
            return inner

        lax.fori_loop(1, nh, push, 0)
        return carry

    lax.fori_loop(0, row_tiles, block, 0)

    push_states(1)

    def keep(s):
        return pltpu.make_async_copy(
            tiles.at[place + s * nh], pot.at[s, pl.ds(place * br, br)], self_sem.at[s]
        )

    for s in range(2):
        keep(s).start()

    far = (nh - 1) * br

    def push_rest(piece):
        count = br // pieces

        def push_one(j, carry):
            send_pot(1, j, piece * count, count).start()
            return carry

        lax.fori_loop(1, nh, push_one, 0)

    def send_term(k, s, first):
        at = pl.ds(half * hr + first, rows)
        return pltpu.make_async_remote_copy(
            src_ref=terms.at[k, s, at],
            dst_ref=terms.at[k, s, at],
            send_sem=term_send.at[k, s],
            recv_sem=term_recv.at[k, s],
            device_id={"build": peer},
            device_id_type=MESH,
        )

    def send_last(s, first):
        return pltpu.make_async_remote_copy(
            src_ref=finals.at[s, pl.ds(first, rows)],
            dst_ref=landed.at[pl.ds(first, rows)],
            send_sem=last_send,
            recv_sem=last_recv,
            device_id={"build": peer},
            device_id_type=MESH,
        )

    def advance(k, s):
        if k == 1:
            others(terms.at[0, s], state_recv.at[s], (nb - 1) * br).wait()
            keep(s).wait()
            others(pot.at[s], pot_recv.at[s], far).wait()
        else:
            others(terms.at[k - 1, s], term_recv.at[k - 1, s], hr).wait()

        def piece(i, carry):
            first = pl.multiple_of(i * rows, rows)
            at = pl.ds(first, rows)
            here = pl.ds(pl.multiple_of(half * hr + first, rows), rows)
            product = jnp.dot(pot[s, at, :], terms[k - 1, s], preferred_element_type=f32) / k
            if k == 1:
                total = terms[0, s, here, :].astype(f32) + product
            else:
                total = summed[s, at, :] + product
            if k < ORDER:
                summed[s, at, :] = total
                terms[k, s, here, :] = product.astype(bf16)
                send_term(k, s, first).start()
            else:
                finals[s, at, :] = total.astype(bf16)

                @pl.when(half != s)
                def _():
                    send_last(s, first).start()

            return carry

        lax.fori_loop(0, hr // rows, piece, 0)

    lead = 3
    push_rest(0)
    for k in range(1, lead + 1):
        advance(k, 0)
        if k < pieces:
            push_rest(k)
    for k in range(1, ORDER + 1):
        advance(k, 1)
        if k + lead <= ORDER:
            advance(k + lead, 0)

    own_half = pl.ds(pl.multiple_of(half * hr, hr), hr)
    out_ref[own_half, :] = finals[half]
    others(landed, last_recv, hr).wait()
    other_half = pl.ds(pl.multiple_of((1 - half) * hr, hr), hr)
    out_ref[other_half, :] = landed[...]
    others(landed, last_send, hr).wait()
    others(sums, sum_recv, npr - 1).wait()
    overall_ref[...] = jnp.sum(sums[...], axis=0)
    others(sums, sum_send, npr - 1).wait()
    others(inverses, inverse_send, nb - 1).wait()
    others(got, got_send, nb - 1).wait()
    others(parts, part_send, nb - 1).wait()
    for s in range(2):
        others(pot.at[s], pot_send.at[s], far).wait()
        others(terms.at[0, s], state_send.at[s], (nb - 1) * br).wait()
        for k in range(1, ORDER):
            others(terms.at[k, s], term_send.at[k, s], hr).wait()


def shards(cholesky, half_vectors, walkers, inverse_intersection, fields, weights, sources):
    nb = lax.axis_size("build")
    npr = lax.axis_size("prop")
    builder = lax.axis_index("build")
    member = lax.axis_index("prop")
    vectors, br, orbitals = cholesky.shape
    electrons = walkers.shape[2]
    hr = orbitals // 2
    wide = vectors * TILE
    lanes = -(-vectors // 128) * 128
    group = min(nb, 8)
    slots = min(SLOTS, br // TILE)
    group_fields = lax.dynamic_index_in_dim(fields.reshape(nb, npr, vectors), member, 1, False)
    group_fields = jnp.pad(group_fields, ((0, 0), (0, lanes - vectors)))
    group_weights = lax.dynamic_index_in_dim(weights.reshape(nb, npr), member, 1, False)
    origin = lax.dynamic_index_in_dim(sources.reshape(nb, npr), member, 1, False) // npr
    choice = (origin[:, None] == jnp.arange(nb, dtype=origin.dtype)[None, :]).astype(bf16)
    vmem = pl.BlockSpec(memory_space=pltpu.VMEM)
    dma = pltpu.SemaphoreType.DMA
    stepped, grown, overall = pl.pallas_call(
        functools.partial(step_kernel, nb, npr),
        out_shape=(
            jax.ShapeDtypeStruct((orbitals, electrons), bf16),
            jax.ShapeDtypeStruct((nb, 1), f32),
            jax.ShapeDtypeStruct((8, 128), f32),
        ),
        in_specs=[vmem] * 6
        + [pl.BlockSpec(memory_space=pltpu.SMEM), pl.BlockSpec(memory_space=pl.ANY)],
        out_specs=(vmem, vmem, vmem),
        scratch_shapes=[
            pltpu.VMEM((nb, br, electrons), bf16),
            pltpu.VMEM((nb,) + inverse_intersection.shape[1:], bf16),
            pltpu.VMEM((nb, br, electrons), bf16),
            pltpu.VMEM((group * TILE, wide), f32),
            pltpu.VMEM((nb, nb, lanes), f32),
            pltpu.VMEM((npr, 8, 128), f32),
            pltpu.VMEM((nb, lanes), f32),
            pltpu.VMEM((nb, br, electrons), bf16),
            pltpu.VMEM((slots, vectors, TILE, orbitals), bf16),
            pltpu.VMEM((nb * TILE, wide), bf16),
            pltpu.VMEM((nb, br, orbitals), bf16),
            pltpu.VMEM((2, hr, orbitals), bf16),
            pltpu.VMEM((ORDER, 2, orbitals, electrons), bf16),
            pltpu.VMEM((2, hr, electrons), f32),
            pltpu.VMEM((2, hr, electrons), bf16),
            pltpu.VMEM((hr, electrons), bf16),
            dma((slots,)),
            dma((2,)),
            dma,
            dma,
            dma,
            dma,
            dma,
            dma,
            dma,
            dma,
            dma((2,)),
            dma((2,)),
            dma((2,)),
            dma((2,)),
            dma((ORDER, 2)),
            dma((ORDER, 2)),
            dma,
            dma,
        ],
        compiler_params=pltpu.CompilerParams(
            collective_id=0, has_side_effects=True, vmem_limit_bytes=60 * 1024 * 1024
        ),
    )(
        walkers[0],
        inverse_intersection[0],
        half_vectors,
        group_fields,
        group_weights[:, None],
        choice,
        origin,
        cholesky,
    )
    own_choice = lax.dynamic_index_in_dim(origin, builder, 0, False)
    kept_weight = lax.dynamic_index_in_dim(grown[:, 0], own_choice, 0, False)
    new_weight = kept_weight * (nb * npr) / overall[0, 0]
    return (stepped[None], new_weight.reshape(1))


def solution(mesh):
    placed = (
        P(None, "build", None),
        P(None, "build", None),
        P(("build", "prop"), None, None),
        P(("build", "prop"), None, None),
        P(),
        P(),
        P(),
    )
    return jax.shard_map(
        shards,
        mesh=mesh,
        in_specs=placed,
        out_specs=(P(("build", "prop"), None, None), P(("build", "prop"))),
        check_vma=False,
    )
```

time: 311 us -> 269 us (0.86)
  blocking collectives: 28 us -> 0 us
  Pallas kernels: 233 us -> 251 us
  waiting for transfers between devices: 14.2 us -> 0 us
  starting transfers between devices: 11.4 us -> 0 us
  local copies, waits for them, and re-layouts: 12.2 us -> 7.19 us
  matrix products: 3.27 us -> 0 us
    psum x2 -> x0, blocking collectives: 28 us -> none  [the longest x1 21.7 us: shards(): force_bias = lax.psum(partial_value, 'build')]
    pallas_call x1, Pallas kernels: 233 us -> 251 us  [shards(): pl.pallas_call(functools.partial(step_kernel, nb, npr), out_shape=(jax.Sh...]
    all_to_all x2 -> x0, waiting for transfers between devices: 14.2 us -> none  [the longest x1 14.2 us: shards(): lax.all_to_all(outgoing[0], 'build', split_axis=1, concat_axis=0, tiled=T...]
    all_to_all x2 -> x0, starting transfers between devices: 11.4 us -> none  [the longest x1 7.28 us: shards(): lax.all_to_all(outgoing[0], 'build', split_axis=1, concat_axis=0, tiled=T...]
    unnamed x10 -> x5, local copies, waits for them, and re-layouts: 6.49 us -> 2.59 us
    dot_general x2 -> x0, matrix products: 3.27 us -> none  [the longest x1 1.95 us: shards(): jnp.einsum('wri,gri->wg', got_theta[:, 0], half_vectors, preferred_elemen...]
  transfers between devices with their start and end apart: 2 -> 0, of which waited for: 1 -> 0; matrix products, arithmetic and copies ran while one was open for 3% -> 0% of each run, Pallas kernels for 0% -> 0%
where the time goes in v2:
time: 269 us; the launch traced here: 265 us
  Pallas kernels  251 us (93%)
  local copies, waits for them, and re-layouts  7.19 us (3%)
  between operations  5.22 us (2%)
    pallas_call x1, Pallas kernels, shards(): pl.pallas_call(functools.partial(step_kernel, nb, npr), out_shape=(jax.Sh...  251 us

profile of v2, /device:TPU:0, one launch (start us, length us, event | category | flops | bytes accessed | tf_op | source)
XLA Modules:
  0.0 265.3 jit_solution(9019355250261560742)
XLA Ops:
  0.6 0.0 copy-start
  0.6 0.7 copy-done
  1.4 0.6 pad.4.fields_ref
  2.0 0.7 reshape.23
  2.7 0.7 constant_dynamic-slice_fusion.1.weights_ref
  3.4 0.7 reshape.24
  4.1 0.2 dynamic-slice_reduce_fusion
  4.3 0.0 copy-start.1
  4.3 0.7 dynamic_slice.23
  7.1 0.6 fusion.3.choice_ref
  7.7 0.0 copy-done.1
  7.7 250.8 %shard_map.86 = (bf16[2048,128]{1,0:T(8,128)(2,1)}, f32[8,1]{1,0:T(8,128)}, f32[8,128]{1,0:T(8,128)}) custom-call(bf16[2048,128]{1,0:T(8,128)(2,1)} %bitcast.10, bf16[128,128]{1,0:T(8,128)(2,1)} %bitcast.12, bf16[48,256,128]{2,1,0:T(8,128)(2,1)} %half_ref.1, f32[8,128]{1,0:T(8,128)} %pad.4.fields_ref, f32[8,1]{1,0:T(8,128)} %constant_dynamic-slice_fusion.1.weights_ref, ...), custom_call_target="tpu_custom_call" | custom-call | tf_op jit(solution)/shard_map/pallas_call | solution.py:419
  258.5 1.2 slice.3
  259.7 1.2 fusion.4
  262.3 1.9 copy.13
  (2 shorter events, 0.0 us)
Async XLA Ops:
  0.6 0.7 copy-start
  4.3 3.4 %copy-start.1 = (s32[8]{0:T(128)}, s32[8]{0:T(128)S(1)}, u32[]{:S(2)}) copy-start(s32[8]{0:T(128)S(1)} %and_select_fusion.origin_ref) | copy-start | bytes 100

commit v3 on v2

--- a/solution.py
+++ b/solution.py
@@ -38,12 +38,14 @@
     half_ref,
     fields_ref,
     weights_ref,
-    choice_ref,
     origin_ref,
     chol_ref,
     out_ref,
+    fresh_ref,
+    drawn_ref,
+    heavy_ref,
+    coeffs_ref,
     grown_ref,
-    overall_ref,
     got,
     inverses,
     theta,
@@ -58,6 +60,7 @@
     pot,
     terms,
     summed,
+    partial,
     finals,
     landed,
     load_sem,
@@ -88,7 +91,7 @@
     vectors, br, orbitals = chol_ref.shape
     electrons = walker_ref.shape[1]
     wide = vectors * TILE
-    lanes = fields_ref.shape[1]
+    lanes = parts.shape[2]
     hr = orbitals // 2
     row_tiles = br // TILE
     slots = chunks.shape[0]
@@ -124,6 +127,13 @@
     own_rows = pl.ds(pl.multiple_of(me * br, br), br)
     got[me] = walker_ref[own_rows, :]
     inverses[me] = inverse_ref[...]
+
+    def collect(v, carry):
+        drawn_ref[pl.ds(v, 1), :] = fields_ref[pl.ds(v * npr + mine, 1), :]
+        heavy_ref[pl.ds(v, 1), :] = jnp.full((1, 128), weights_ref[v * npr + mine], f32)
+        return carry
+
+    lax.fori_loop(0, nb, collect, 0)
     pl.semaphore_wait(barrier, nb - 1 + npr - 1)
 
     def share(j, carry):
@@ -152,7 +162,7 @@
 
     def rotate(v, carry):
         theta[v] = jnp.dot(got[v], inverses[v], preferred_element_type=f32).astype(bf16)
-        starts_ref[v] = got[origin_ref[v]]
+        starts_ref[v] = got[lax.div(origin_ref[v * npr + mine], npr)]
         return carry
 
     lax.fori_loop(0, nb, rotate, 0)
@@ -223,9 +233,10 @@
     force_bias = lax.fori_loop(
         1, nb, lambda j, held: held + parts[j], parts[0]
     )
-    drawn = fields_ref[...]
+    force_bias = force_bias[:, :vectors]
+    drawn = drawn_ref[...]
     exponent = jnp.sum(force_bias * (drawn - 0.5 * force_bias), axis=-1, keepdims=True)
-    grown = weights_ref[...] * jnp.exp(exponent)
+    grown = heavy_ref[...] * jnp.exp(exponent)
     grown_ref[...] = grown
     sums[mine] = jnp.broadcast_to(jnp.sum(grown, axis=0, keepdims=True), sums.shape[1:])
     for j in range(1, npr):
@@ -237,8 +248,13 @@
             device_id={"prop": lax.rem(mine + j, npr)},
             device_id_type=MESH,
         ).start()
-    coeffs = (drawn - force_bias).astype(bf16)
-    picked_ref[...] = jnp.dot(choice_ref[...], coeffs, preferred_element_type=f32)
+    coeffs_ref[...] = drawn - force_bias
+
+    def pick(v, carry):
+        picked_ref[pl.ds(v, 1), :] = coeffs_ref[pl.ds(lax.div(origin_ref[v * npr + mine], npr), 1), :]
+        return carry
+
+    lax.fori_loop(0, nb, pick, 0)
 
     def fill(v, carry):
         c = picked_ref[pl.ds(pl.multiple_of(v * group, group), group), :].astype(bf16)
@@ -335,6 +351,9 @@
             device_id_type=MESH,
         )
 
+    own_half = pl.ds(pl.multiple_of(half * hr, hr), hr)
+    other_half = pl.ds(pl.multiple_of((1 - half) * hr, hr), hr)
+
     def advance(k, s):
         if k == 1:
             others(terms.at[0, s], state_recv.at[s], (nb - 1) * br).wait()
@@ -347,7 +366,14 @@
             first = pl.multiple_of(i * rows, rows)
             at = pl.ds(first, rows)
             here = pl.ds(pl.multiple_of(half * hr + first, rows), rows)
-            product = jnp.dot(pot[s, at, :], terms[k - 1, s], preferred_element_type=f32) / k
+            if k == 1:
+                product = jnp.dot(pot[s, at, :], terms[0, s], preferred_element_type=f32)
+            else:
+                product = partial[s, at, :] + jnp.dot(
+                    pot[s, at, other_half], terms[k - 1, s, other_half, :],
+                    preferred_element_type=f32,
+                )
+            product = product / k
             if k == 1:
                 total = terms[0, s, here, :].astype(f32) + product
             else:
@@ -367,6 +393,16 @@
 
         lax.fori_loop(0, hr // rows, piece, 0)
 
+        def ahead(i, carry):
+            at = pl.ds(pl.multiple_of(i * rows, rows), rows)
+            partial[s, at, :] = jnp.dot(
+                pot[s, at, own_half], terms[k, s, own_half, :], preferred_element_type=f32
+            )
+            return carry
+
+        if k < ORDER:
+            lax.fori_loop(0, hr // rows, ahead, 0)
+
     lead = 3
     push_rest(0)
     for k in range(1, lead + 1):
@@ -378,14 +414,13 @@
         if k + lead <= ORDER:
             advance(k + lead, 0)
 
-    own_half = pl.ds(pl.multiple_of(half * hr, hr), hr)
     out_ref[own_half, :] = finals[half]
     others(landed, last_recv, hr).wait()
-    other_half = pl.ds(pl.multiple_of((1 - half) * hr, hr), hr)
     out_ref[other_half, :] = landed[...]
     others(landed, last_send, hr).wait()
     others(sums, sum_recv, npr - 1).wait()
-    overall_ref[...] = jnp.sum(sums[...], axis=0)
+    kept = grown_ref[pl.ds(lax.div(origin_ref[me * npr + mine], npr), 1), :]
+    fresh_ref[...] = kept * (nb * npr) / jnp.sum(sums[...], axis=0)[0:1, :]
     others(sums, sum_send, npr - 1).wait()
     others(inverses, inverse_send, nb - 1).wait()
     others(got, got_send, nb - 1).wait()
@@ -400,8 +435,6 @@
 def shards(cholesky, half_vectors, walkers, inverse_intersection, fields, weights, sources):
     nb = lax.axis_size("build")
     npr = lax.axis_size("prop")
-    builder = lax.axis_index("build")
-    member = lax.axis_index("prop")
     vectors, br, orbitals = cholesky.shape
     electrons = walkers.shape[2]
     hr = orbitals // 2
@@ -409,37 +442,37 @@
     lanes = -(-vectors // 128) * 128
     group = min(nb, 8)
     slots = min(SLOTS, br // TILE)
-    group_fields = lax.dynamic_index_in_dim(fields.reshape(nb, npr, vectors), member, 1, False)
-    group_fields = jnp.pad(group_fields, ((0, 0), (0, lanes - vectors)))
-    group_weights = lax.dynamic_index_in_dim(weights.reshape(nb, npr), member, 1, False)
-    origin = lax.dynamic_index_in_dim(sources.reshape(nb, npr), member, 1, False) // npr
-    choice = (origin[:, None] == jnp.arange(nb, dtype=origin.dtype)[None, :]).astype(bf16)
     vmem = pl.BlockSpec(memory_space=pltpu.VMEM)
     dma = pltpu.SemaphoreType.DMA
-    stepped, grown, overall = pl.pallas_call(
+    stepped, fresh = pl.pallas_call(
         functools.partial(step_kernel, nb, npr),
         out_shape=(
             jax.ShapeDtypeStruct((orbitals, electrons), bf16),
-            jax.ShapeDtypeStruct((nb, 1), f32),
-            jax.ShapeDtypeStruct((8, 128), f32),
+            jax.ShapeDtypeStruct((1, 128), f32),
         ),
-        in_specs=[vmem] * 6
-        + [pl.BlockSpec(memory_space=pltpu.SMEM), pl.BlockSpec(memory_space=pl.ANY)],
-        out_specs=(vmem, vmem, vmem),
+        in_specs=[vmem] * 4
+        + [pl.BlockSpec(memory_space=pltpu.SMEM)] * 2
+        + [pl.BlockSpec(memory_space=pl.ANY)],
+        out_specs=(vmem, vmem),
         scratch_shapes=[
+            pltpu.VMEM((nb, vectors), f32),
+            pltpu.VMEM((nb, 128), f32),
+            pltpu.VMEM((nb, vectors), f32),
+            pltpu.VMEM((nb, 128), f32),
             pltpu.VMEM((nb, br, electrons), bf16),
             pltpu.VMEM((nb,) + inverse_intersection.shape[1:], bf16),
             pltpu.VMEM((nb, br, electrons), bf16),
             pltpu.VMEM((group * TILE, wide), f32),
             pltpu.VMEM((nb, nb, lanes), f32),
             pltpu.VMEM((npr, 8, 128), f32),
-            pltpu.VMEM((nb, lanes), f32),
+            pltpu.VMEM((nb, vectors), f32),
             pltpu.VMEM((nb, br, electrons), bf16),
             pltpu.VMEM((slots, vectors, TILE, orbitals), bf16),
             pltpu.VMEM((nb * TILE, wide), bf16),
             pltpu.VMEM((nb, br, orbitals), bf16),
             pltpu.VMEM((2, hr, orbitals), bf16),
             pltpu.VMEM((ORDER, 2, orbitals, electrons), bf16),
+            pltpu.VMEM((2, hr, electrons), f32),
             pltpu.VMEM((2, hr, electrons), f32),
             pltpu.VMEM((2, hr, electrons), bf16),
             pltpu.VMEM((hr, electrons), bf16),
@@ -469,16 +502,12 @@
         walkers[0],
         inverse_intersection[0],
         half_vectors,
-        group_fields,
-        group_weights[:, None],
-        choice,
-        origin,
+        fields,
+        weights,
+        sources,
         cholesky,
     )
-    own_choice = lax.dynamic_index_in_dim(origin, builder, 0, False)
-    kept_weight = lax.dynamic_index_in_dim(grown[:, 0], own_choice, 0, False)
-    new_weight = kept_weight * (nb * npr) / overall[0, 0]
-    return (stepped[None], new_weight.reshape(1))
+    return (stepped[None], fresh[0, :1])
 
 
 def solution(mesh):

time: 269 us -> 259 us (0.963)
  local copies, waits for them, and re-layouts: 7.19 us -> 1.87 us
  between operations: 5.22 us -> 2.34 us
where the time goes in v3:
time: 259 us; the launch traced here: 255 us
  Pallas kernels  251 us (97%)
    pallas_call x1, Pallas kernels, shards(): pl.pallas_call(functools.partial(step_kernel, nb, npr), out_shape=(jax.Sh...  251 us

profile of v3, /device:TPU:0, one launch (start us, length us, event | category | flops | bytes accessed | tf_op | source)
XLA Modules:
  0.0 254.9 jit_solution(15004871591839179513)
XLA Ops:
  0.6 250.6 %shard_map.86 = (bf16[2048,128]{1,0:T(8,128)(2,1)}, f32[1,128]{1,0:T(1,128)}) custom-call(bf16[2048,128]{1,0:T(8,128)(2,1)} %bitcast.5, bf16[128,128]{1,0:T(8,128)(2,1)} %bitcast.7, bf16[48,256,128]{2,1,0:T(8,128)(2,1)} %half_ref.1, f32[32,48]{1,0:T(8,128)} %fields_ref.1, f32[32]{0:T(128)} %weights_ref.1, s32[32]{0:T(128)} %origin_ref.1, ...), custom_call_target="tpu_custom_call" | custom-call | tf_op jit(solution)/shard_map/pallas_call | solution.py:447
  251.3 1.9 copy.11

commit v4 on v3

--- a/solution.py
+++ b/solution.py
@@ -404,11 +404,21 @@
             lax.fori_loop(0, hr // rows, ahead, 0)
 
     lead = 3
-    push_rest(0)
+    early = lax.rem(mine, 2) == 1
+
+    @pl.when(early)
+    def _():
+        for piece in range(pieces):
+            push_rest(piece)
+
     for k in range(1, lead + 1):
         advance(k, 0)
-        if k < pieces:
-            push_rest(k)
+
+        @pl.when(jnp.logical_not(early))
+        def _():
+            for piece in range(pieces * (k - 1) // lead, pieces * k // lead):
+                push_rest(piece)
+
     for k in range(1, ORDER + 1):
         advance(k, 1)
         if k + lead <= ORDER:

time: 259 us -> 257 us (level)
  no operation moved by 1% of the time
where the time goes in v4:
time: 257 us; the launch traced here: 254 us
  Pallas kernels  250 us (97%)
    pallas_call x1, Pallas kernels, shards(): pl.pallas_call(functools.partial(step_kernel, nb, npr), out_shape=(jax.Sh...  250 us

profile of v4, /device:TPU:0, one launch (start us, length us, event | category | flops | bytes accessed | tf_op | source)
XLA Modules:
  0.0 253.7 jit_solution(18211213203501214751)
XLA Ops:
  0.6 249.5 %shard_map.86 = (bf16[2048,128]{1,0:T(8,128)(2,1)}, f32[1,128]{1,0:T(1,128)}) custom-call(bf16[2048,128]{1,0:T(8,128)(2,1)} %bitcast.5, bf16[128,128]{1,0:T(8,128)(2,1)} %bitcast.7, bf16[48,256,128]{2,1,0:T(8,128)(2,1)} %half_ref.1, f32[32,48]{1,0:T(8,128)} %fields_ref.1, f32[32]{0:T(128)} %weights_ref.1, s32[32]{0:T(128)} %origin_ref.1, ...), custom_call_target="tpu_custom_call" | custom-call | tf_op jit(solution)/shard_map/pallas_call | solution.py:457
  250.2 1.9 copy.11
